TPU v7x, 128 devices: a whole 4x4x4 slice. The times are simulated.
128 devices in a mesh: dp: 8 (over x_hi, z), tensor: 16 (over x_lo, y, core).
Axes of the slice: x: 4 (x_hi: 2, x_lo: 2; x = x_hi * 2 + x_lo), y: 4, z: 4, core: 2. Of those that a mesh axis runs over, the one named last changes fastest.
Arguments:
- ckpt_values: bfloat16 [2048, 18432], P(('dp', 'tensor')), may hold values from -6 to 6
- ckpt_scales: bfloat16 [2048, 144], P(('dp', 'tensor')), may hold values from 0.25 to 4
- norm_gain: float32 [18432], replicated, may hold values from 0.5 to 1.5
- pre_act: bfloat16 [2048, 36864], P('dp', 'tensor'), may hold values from -6 to 6
- act_grad: bfloat16 [2048, 36864], P('dp', 'tensor'), may hold values from -0.09375 to 0.09375
Outputs:
- weight_grad: bfloat16 [18432, 36864], P('dp', 'tensor')
All inputs are finite; a program needn't handle non-finite values.
Results may differ from a plain program's by a relative error of at most 0.0057.
Values may be sent and summed in bfloat16 or wider, within the bound.
A program may use at most 128 MiB of HBM per device.

v0:
```python
import jax
import jax.numpy as jnp
from jax import lax
from jax.sharding import PartitionSpec as P

QB = 128


def normalize(values, scales, gain):
    count = values.shape[0]
    width = values.shape[1]
    inputs = (
        values.astype(jnp.float32).reshape(count, width // QB, QB)
        * scales.astype(jnp.float32)[:, :, None]
    )
    inputs = inputs.reshape(count, width)
    inverse = lax.rsqrt(jnp.mean(inputs * inputs, axis=1, keepdims=True) + 1e-05)
    return (inputs * inverse * gain).astype(jnp.bfloat16)


def on_device(ckpt_values, ckpt_scales, norm_gain, pre_act, act_grad):
    pre_grad = (
        act_grad.astype(jnp.float32) * 2.0 * jnp.maximum(pre_act.astype(jnp.float32), 0.0)
    ).astype(jnp.bfloat16)
    normed = normalize(ckpt_values, ckpt_scales, norm_gain)
    gathered = lax.all_gather(normed, "tensor", axis=0, tiled=True)
    grouped = lax.all_to_all(gathered[None], "dp", split_axis=2, concat_axis=0, tiled=True)
    features = grouped.reshape(grouped.shape[0] * grouped.shape[1], grouped.shape[2])
    total = lax.dot_general(
        features,
        lax.all_gather(pre_grad, "dp", axis=0, tiled=True),
        (((0,), (0,)), ((), ())),
        preferred_element_type=jnp.float32,
    )
    return total.astype(jnp.bfloat16)


def solution(mesh):
    in_specs = (
        P(("dp", "tensor"), None),
        P(("dp", "tensor"), None),
        P(),
        P("dp", "tensor"),
        P("dp", "tensor"),
    )
    out_specs = P("dp", "tensor")
    return jax.shard_map(
        on_device, mesh=mesh, in_specs=in_specs, out_specs=out_specs, check_vma=False
    )
```

profile of v0, /device:TPU:0, one launch (start us, length us, event | category | flops | bytes accessed | tf_op | source)
XLA Modules:
  0.0 405.1 jit_solution(7969495020714175538)
XLA Ops:
  6.5 0.0 copy-start
  6.5 0.0 copy-start.3
  6.5 0.0 all-gather.3.cloned.1.call-start
  6.5 1.1 mul.39
  7.7 0.0 copy-start.1
  7.7 0.0 copy-start.2
  7.7 1.7 multiply_reduce_fusion
  9.4 0.0 copy-done
  9.4 0.0 copy-done.3
  9.4 1.3 multiply_convert_fusion.1
  10.7 0.0 all-gather.3.cloned.1.call-update
  10.7 0.0 all-gather.5.cloned.1.call-start
  10.7 0.0 copy-done.1
  10.8 0.0 copy-done.2
  10.8 1.5 multiply_convert_fusion
  12.2 0.0 all-gather.5.cloned.1.call-update
  12.2 58.1 %all-gather.3.cloned.1.call-done = bf16[256,18432]{1,0:T(8,128)(2,1)} async-done(((bf16[16,18432]{1,0:T(8,128)(2,1)}), bf16[256,18432]{1,0:T(8,128)(2,1)}) %all-gather.3.cloned.1.call-update) | async-done | bytes 9437200 | tf_op jit(solution)/shard_map/all_gather | solution.py:26
  70.3 38.5 %copy.9 = bf16[1,256,18432]{1,0,2:T(2,128)(2,1)} copy(bf16[1,256,18432]{2,1,0:T(8,128)(2,1)} %bitcast.21) | data formatting | bytes 18874368 | tf_op jit(solution)/shard_map/broadcast_in_dim | solution.py:27
  108.8 0.5 broadcast.24
  109.4 95.0 %reduce = bf16[18432,256]{1,0:T(8,128)(2,1)} reduce(bf16[18432,1,256]{2,1,0:T(2,128)(2,1)} %bitcast.17, bf16[]{:T(256)} %broadcast.24), dimensions={1}, to_apply=%bitcast.12.reduce_sub_computation | reduce | bytes 18874370
  204.4 10.4 %reshape.18 = bf16[8,2,294912]{2,1,0:T(2,128)(2,1)} reshape(bf16[18432,256]{1,0:T(8,128)(2,1)} %reduce) | data formatting | bytes 18874368
  214.8 114.4 %all_to_all.15 = bf16[8,2,294912]{2,1,0:T(2,128)(2,1)} all-to-all(bf16[8,2,294912]{2,1,0:T(2,128)(2,1)} %reshape.18), channel_id=1, replica_groups=mesh['dp'=8,'tensor'=16] {'dp'}, dimensions={0} | all-to-all | bytes 18874368 | tf_op jit(solution)/shard_map/all_to_all | solution.py:27
  329.2 14.5 %reshape.19 = bf16[18432,1,256]{2,1,0:T(2,128)(2,1)} reshape(bf16[8,2,294912]{2,1,0:T(2,128)(2,1)} %all_to_all.15) | data formatting | bytes 18874368
  343.7 12.7 %copy.11 = bf16[1,256,18432]{1,2,0:T(8,128)(2,1)} copy(bf16[1,256,18432]{1,0,2:T(2,128)(2,1)} %bitcast.16) | data formatting | bytes 18874368
  356.4 12.6 %copy.10 = bf16[8,1,256,2304]{3,2,0,1:T(8,128)(2,1)} copy(bf16[8,1,256,2304]{2,3,0,1:T(8,128)(2,1)} %bitcast.18) | data formatting | bytes 18874368 | tf_op jit(solution)/shard_map/all_to_all | solution.py:27
  369.0 0.0 all-gather.5.cloned.1.call-done
  369.0 29.3 %convolution_convert_fusion = bf16[2304,2304]{1,0:T(8,128)(2,1)} fusion(bf16[2048,2304]{1,0:T(8,128)(2,1)} %bitcast.22, bf16[2048,2304]{1,0:T(8,128)(2,1)} %all-gather.5.cloned.1.call-done), kind=kOutput, calls=%fused_computation | convolution fusion | flops 21748580352 | bytes 29491200 | tf_op jit(solution)/shard_map/dot_general | solution.py:29
  (1 shorter events, 0.0 us)
Async XLA Ops:
  6.5 2.9 copy-start
  6.5 2.9 copy-start.3
  6.5 63.8 %all-gather.3.cloned.1.call-start = ((), (), s32[]{:S(2)}) async-start(), calls=%async_computation.1 | async-start | bytes 10027008 | tf_op jit(solution)/shard_map/all_gather | solution.py:26
  7.7 3.1 copy-start.1
  7.7 3.1 copy-start.2
  10.7 358.3 %all-gather.5.cloned.1.call-start = ((), (), s32[]{:S(2)}) async-start(), calls=%async_computation.2 | async-start | bytes 10616832 | tf_op jit(solution)/shard_map/all_gather | solution.py:31
Sparse Core Ops, SparseCore 0:
  10.8 59.4 all-gather.2
  72.6 117.6 all-gather.4
where the time goes:
time: 407 us; the launch traced here: 405 us
  blocking collectives  114 us (28%)
  other arithmetic  99.5 us (24%)
  local copies, waits for them, and re-layouts  90.3 us (22%)
  waiting for transfers between devices  58.1 us (14%)
  matrix products  29.3 us (7%)
  between operations  13.5 us (3%)
    all_to_all x1, blocking collectives, on_device(): lax.all_to_all(gathered[None], 'dp', split_axis=2, concat_axis=0, tiled=T...  114 us
    unnamed x1, other arithmetic  95 us
    all_gather x1, waiting for transfers between devices, on_device(): gathered = lax.all_gather(normed, 'tensor', axis=0, tiled=True)  58.1 us
    broadcast_in_dim x1, local copies, waits for them, and re-layouts, on_device(): gathered[None]  38.5 us
    unnamed x12, local copies, waits for them, and re-layouts  38.1 us
    dot_general x1, matrix products, on_device(): lax.dot_general(features, lax.all_gather(pre_grad, 'dp', axis=0, tiled=Tr...  29.3 us
    all_to_all x1, local copies, waits for them, and re-layouts, on_device(): lax.all_to_all(gathered[None], 'dp', split_axis=2, concat_axis=0, tiled=T...  12.6 us
  transfers between devices with their start and end apart: 2, of which 1 were waited for; matrix products, arithmetic and copies ran while one was open for 46% of the time, Pallas kernels for 0%

commit v1 on v0

--- a/solution.py
+++ b/solution.py
@@ -23,7 +23,10 @@
         act_grad.astype(jnp.float32) * 2.0 * jnp.maximum(pre_act.astype(jnp.float32), 0.0)
     ).astype(jnp.bfloat16)
     normed = normalize(ckpt_values, ckpt_scales, norm_gain)
-    gathered = lax.all_gather(normed, "tensor", axis=0, tiled=True)
+    n_dev = lax.axis_size("tensor")
+    blocks = jnp.stack([normed for _ in range(n_dev)])
+    blocks = lax.all_to_all(blocks, "tensor", split_axis=0, concat_axis=0)
+    gathered = jnp.concatenate(blocks, axis=0)
     grouped = lax.all_to_all(gathered[None], "dp", split_axis=2, concat_axis=0, tiled=True)
     features = grouped.reshape(grouped.shape[0] * grouped.shape[1], grouped.shape[2])
     total = lax.dot_general(

time: 407 us -> 545 us (1.34); the launches traced: 405 us -> 535 us
  waiting for transfers between devices: 58.1 us -> 177 us
  starting transfers between devices: 0.04 us -> 5.8 us
    all_to_all x0 -> x1, waiting for transfers between devices: none -> 177 us  [on_device(): blocks = lax.all_to_all(blocks, 'tensor', split_axis=0, concat_axis=0)]
    all_gather x1 -> x0, waiting for transfers between devices: 58.1 us -> none  [on_device(): gathered = lax.all_gather(normed, 'tensor', axis=0, tiled=True)]
    another operation x0 -> x2, local copies, waits for them, and re-layouts: none -> 43.1 us  [the longest x1 38.3 us: on_device(): gathered[None]]
    broadcast_in_dim x1 -> x0, local copies, waits for them, and re-layouts: 38.5 us -> none  [on_device(): gathered[None]]
    all_to_all x0 -> x1, starting transfers between devices: none -> 5.76 us  [on_device(): blocks = lax.all_to_all(blocks, 'tensor', split_axis=0, concat_axis=0)]
  transfers between devices with their start and end apart: 2 -> 2, of which waited for: 1 -> 1; matrix products, arithmetic and copies ran while one was open for 46% -> 35% of each run, Pallas kernels for 0% -> 0%
where the time goes in v1:
time: 545 us; the launch traced here: 535 us
  waiting for transfers between devices  177 us (32%)
  blocking collectives  115 us (21%)
  other arithmetic  98.4 us (18%)
  local copies, waits for them, and re-layouts  95.2 us (17%)
  matrix products  29.3 us (5%)
  between operations  13.5 us (2%)
  starting transfers between devices  5.8 us (1%)
    all_to_all x1, waiting for transfers between devices, on_device(): blocks = lax.all_to_all(blocks, 'tensor', split_axis=0, concat_axis=0)  177 us
    all_to_all x1, blocking collectives, on_device(): lax.all_to_all(gathered[None], 'dp', split_axis=2, concat_axis=0, tiled=T...  115 us
    unnamed x1, other arithmetic  95 us
    another operation x1, local copies, waits for them, and re-layouts, on_device(): gathered[None]  38.3 us
    unnamed x12, local copies, waits for them, and re-layouts  38.1 us
    dot_general x1, matrix products, on_device(): lax.dot_general(features, lax.all_gather(pre_grad, 'dp', axis=0, tiled=Tr...  29.3 us
    all_to_all x1, local copies, waits for them, and re-layouts, on_device(): lax.all_to_all(gathered[None], 'dp', split_axis=2, concat_axis=0, tiled=T...  12.9 us
  transfers between devices with their start and end apart: 2, of which 1 were waited for; matrix products, arithmetic and copies ran while one was open for 35% of the time, Pallas kernels for 0%

profile of v1, /device:TPU:0, one launch (start us, length us, event | category | flops | bytes accessed | tf_op | source)
XLA Modules:
  0.0 534.6 jit_solution(686122364017184653)
XLA Ops:
  6.5 0.0 copy-start
  6.5 0.0 copy-start.3
  6.5 1.1 mul.39
  7.7 1.6 multiply_reduce_fusion
  9.2 0.0 copy-done
  9.2 0.0 copy-done.3
  9.2 0.4 multiply_convert_fusion.1
  9.7 4.8 stack.2
  14.5 0.0 copy-start.1
  14.5 0.0 copy-start.2
  14.5 5.8 %all-to-all-start = ((bf16[16,16,18432]{2,1,0:T(8,128)(2,1)}), bf16[16,16,18432]{2,1,0:T(8,128)(2,1)}, u32[]{:S(2)}, u32[]{:S(2)}) async-start(bf16[16,16,18432]{2,1,0:T(8,128)(2,1)} %stack.2), calls=%async_computation | async-start | bytes 18874368 | tf_op jit(solution)/shard_map/all_to_all | solution.py:28
  20.2 0.0 all-gather.2.cloned.1.call-start
  20.3 0.0 copy-done.1
  20.3 0.0 copy-done.2
  20.3 1.4 multiply_convert_fusion
  21.7 0.0 all-gather.2.cloned.1.call-update
  21.8 177.4 %all-to-all-done = bf16[16,16,18432]{2,1,0:T(8,128)(2,1)} async-done(((bf16[16,16,18432]{2,1,0:T(8,128)(2,1)}), bf16[16,16,18432]{2,1,0:T(8,128)(2,1)}, u32[]{:S(2)}, u32[]{:S(2)}) %all-to-all-start) | async-done | bytes 9437216 | tf_op jit(solution)/shard_map/all_to_all | solution.py:28
  199.2 38.3 %copy.10 = bf16[1,256,18432]{1,0,2:T(2,128)(2,1)} copy(bf16[1,256,18432]{2,1,0:T(8,128)(2,1)} %bitcast) | data formatting | bytes 18874368 | tf_op jit(solution)/shard_map/broadcast_in_dim;reshape | solution.py:30
  237.5 0.5 broadcast.26
  237.9 95.0 %reduce = bf16[18432,256]{1,0:T(8,128)(2,1)} reduce(bf16[18432,1,256]{2,1,0:T(2,128)(2,1)} %bitcast.17, bf16[]{:T(256)} %broadcast.26), dimensions={1}, to_apply=%bitcast.12.reduce_sub_computation | reduce | bytes 18874370
  332.9 10.4 %reshape.20 = bf16[8,2,294912]{2,1,0:T(2,128)(2,1)} reshape(bf16[18432,256]{1,0:T(8,128)(2,1)} %reduce) | data formatting | bytes 18874368
  343.3 115.1 %all_to_all.20 = bf16[8,2,294912]{2,1,0:T(2,128)(2,1)} all-to-all(bf16[8,2,294912]{2,1,0:T(2,128)(2,1)} %reshape.20), channel_id=1, replica_groups=mesh['dp'=8,'tensor'=16] {'dp'}, dimensions={0} | all-to-all | bytes 18874368 | tf_op jit(solution)/shard_map/all_to_all | solution.py:30
  458.4 14.5 %reshape.21 = bf16[18432,1,256]{2,1,0:T(2,128)(2,1)} reshape(bf16[8,2,294912]{2,1,0:T(2,128)(2,1)} %all_to_all.20) | data formatting | bytes 18874368
  472.9 12.7 %copy.12 = bf16[1,256,18432]{1,2,0:T(8,128)(2,1)} copy(bf16[1,256,18432]{1,0,2:T(2,128)(2,1)} %bitcast.16) | data formatting | bytes 18874368
  485.7 12.9 %copy.11 = bf16[8,1,256,2304]{3,2,0,1:T(8,128)(2,1)} copy(bf16[8,1,256,2304]{2,3,0,1:T(8,128)(2,1)} %bitcast.18) | data formatting | bytes 18874368 | tf_op jit(solution)/shard_map/all_to_all | solution.py:30
  498.5 0.0 all-gather.2.cloned.1.call-done
  498.5 29.3 %convolution_convert_fusion = bf16[2304,2304]{1,0:T(8,128)(2,1)} fusion(bf16[2048,2304]{1,0:T(8,128)(2,1)} %bitcast.21, bf16[2048,2304]{1,0:T(8,128)(2,1)} %all-gather.2.cloned.1.call-done), kind=kOutput, calls=%fused_computation | convolution fusion | flops 21748580352 | bytes 29491200 | tf_op jit(solution)/shard_map/dot_general | solution.py:32
  (1 shorter events, 0.0 us)
Async XLA Ops:
  6.5 2.7 copy-start
  6.5 2.7 copy-start.3
  14.5 5.8 %copy-start.1 = (bf16[256,2304]{1,0:T(8,128)(2,1)S(1)}, bf16[256,2304]{1,0:T(8,128)(2,1)}, u32[]{:S(2)}) copy-start(bf16[256,2304]{1,0:T(8,128)(2,1)} %param.8) | copy-start | bytes 3538948
  14.5 5.8 %copy-start.2 = (bf16[256,2304]{1,0:T(8,128)(2,1)S(1)}, bf16[256,2304]{1,0:T(8,128)(2,1)}, u32[]{:S(2)}) copy-start(bf16[256,2304]{1,0:T(8,128)(2,1)} %param.9) | copy-start | bytes 3538948
  14.5 184.7 %all-to-all-start = ((bf16[16,16,18432]{2,1,0:T(8,128)(2,1)}), bf16[16,16,18432]{2,1,0:T(8,128)(2,1)}, u32[]{:S(2)}, u32[]{:S(2)}) async-start(bf16[16,16,18432]{2,1,0:T(8,128)(2,1)} %stack.2), calls=%async_computation | async-start | bytes 18874368 | tf_op jit(solution)/shard_map/all_to_all | solution.py:28
  20.2 478.3 %all-gather.2.cloned.1.call-start = ((), (), s32[]{:S(2)}) async-start(), calls=%async_computation.2 | async-start | bytes 10616832 | tf_op jit(solution)/shard_map/all_gather | solution.py:34
Sparse Core Ops, SparseCore 0:
  23.4 182.9 all-gather.1

commit v2 on v0

--- a/solution.py
+++ b/solution.py
@@ -4,6 +4,13 @@
 from jax.sharding import PartitionSpec as P
 
 QB = 128
+
+
+def exchange_blocks(x, axis, split, join):
+    peers = lax.axis_size(axis)
+    blocks = jnp.stack(jnp.split(x, peers, axis=split), axis=0)
+    blocks = lax.all_to_all(blocks, axis, split_axis=0, concat_axis=0)
+    return jnp.concatenate(blocks, axis=join)
 
 
 def normalize(values, scales, gain):
@@ -24,7 +31,7 @@
     ).astype(jnp.bfloat16)
     normed = normalize(ckpt_values, ckpt_scales, norm_gain)
     gathered = lax.all_gather(normed, "tensor", axis=0, tiled=True)
-    grouped = lax.all_to_all(gathered[None], "dp", split_axis=2, concat_axis=0, tiled=True)
+    grouped = exchange_blocks(gathered[None], "dp", 2, 0)
     features = grouped.reshape(grouped.shape[0] * grouped.shape[1], grouped.shape[2])
     total = lax.dot_general(
         features,

time: 407 us -> 328 us (0.81)
  waiting for transfers between devices: 58.1 us -> 254 us
  blocking collectives: 114 us -> 0 us
  other arithmetic: 99.5 us -> 6.96 us
  local copies, waits for them, and re-layouts: 90.3 us -> 15.8 us
  starting transfers between devices: 0.04 us -> 6.88 us
    all_gather x1, waiting for transfers between devices: 0.01 us -> 198 us  [on_device(): lax.all_gather(pre_grad, 'dp', axis=0, tiled=True)]
    all_to_all x1 -> x0, blocking collectives: 114 us -> none  [on_device(): lax.all_to_all(gathered[None], 'dp', split_axis=2, concat_axis=0, tiled=T...]
    unnamed x1 -> x0, other arithmetic: 95 us -> none
    broadcast_in_dim x1 -> x0, local copies, waits for them, and re-layouts: 38.5 us -> none  [on_device(): gathered[None]]
    unnamed x12 -> x9, local copies, waits for them, and re-layouts: 38.1 us -> 13.7 us
    all_to_all x1 -> x0, local copies, waits for them, and re-layouts: 12.6 us -> none  [on_device(): lax.all_to_all(gathered[None], 'dp', split_axis=2, concat_axis=0, tiled=T...]
    all_to_all x0 -> x1, starting transfers between devices: none -> 6.84 us  [exchange_blocks(): blocks = lax.all_to_all(blocks, axis, split_axis=0, concat_axis=0)]
  transfers between devices with their start and end apart: 2 -> 3, of which waited for: 1 -> 2; matrix products, arithmetic and copies ran while one was open for 46% -> 5% of each run, Pallas kernels for 0% -> 0%
where the time goes in v2:
time: 328 us; the launch traced here: 327 us
  waiting for transfers between devices  254 us (77%)
  matrix products  29.3 us (9%)
  local copies, waits for them, and re-layouts  15.8 us (5%)
  between operations  13.4 us (4%)
  other arithmetic  6.96 us (2%)
  starting transfers between devices  6.88 us (2%)
    all_gather x1, waiting for transfers between devices, on_device(): lax.all_gather(pre_grad, 'dp', axis=0, tiled=True)  198 us
    all_gather x1, waiting for transfers between devices, on_device(): gathered = lax.all_gather(normed, 'tensor', axis=0, tiled=True)  56.5 us
    dot_general x1, matrix products, on_device(): lax.dot_general(features, lax.all_gather(pre_grad, 'dp', axis=0, tiled=Tr...  29.3 us
    unnamed x9, local copies, waits for them, and re-layouts  13.7 us
    all_to_all x1, starting transfers between devices, exchange_blocks(): blocks = lax.all_to_all(blocks, axis, split_axis=0, concat_axis=0)  6.84 us
  transfers between devices with their start and end apart: 3, of which 2 were waited for; matrix products, arithmetic and copies ran while one was open for 5% of the time, Pallas kernels for 0%

profile of v2, /device:TPU:0, one launch (start us, length us, event | category | flops | bytes accessed | tf_op | source)
XLA Modules:
  0.0 326.8 jit_solution(11213551635989437401)
XLA Ops:
  6.5 0.0 all-gather.3.cloned.1.call-start
  6.5 1.1 mul.39
  7.6 1.6 multiply_reduce_fusion
  9.2 2.3 multiply_convert_fusion.1
  11.5 0.0 all-gather.3.cloned.1.call-update
  11.5 0.0 all-gather.5.cloned.1.call-start
  11.6 3.1 multiply_convert_fusion
  14.6 0.0 all-gather.5.cloned.1.call-update
  14.7 56.5 %all-gather.3.cloned.1.call-done = bf16[256,18432]{1,0:T(8,128)(2,1)} async-done(((bf16[16,18432]{1,0:T(8,128)(2,1)}), bf16[256,18432]{1,0:T(8,128)(2,1)}) %all-gather.3.cloned.1.call-update) | async-done | bytes 9437200 | tf_op jit(solution)/shard_map/all_gather | solution.py:33
  71.2 0.0 copy-start
  71.2 2.5 fusion.7
  73.7 3.1 fusion.6
  76.8 2.4 fusion.5
  79.1 2.4 fusion.4
  81.5 0.0 copy-done
  81.5 1.1 fusion.3
  82.6 1.1 fusion.2
  83.7 1.1 fusion.1
  84.8 1.1 fusion
  85.9 6.8 %all-to-all-start = ((bf16[8,1,256,2304]{3,2,1,0:T(8,128)(2,1)}), bf16[8,1,256,2304]{3,2,1,0:T(8,128)(2,1)}, u32[]{:S(2)}, u32[]{:S(2)}) async-start(bf16[8,1,256,2304]{3,2,1,0:T(8,128)(2,1)} %fusion), calls=%async_computation | async-start | bytes 18874368 | tf_op jit(solution)/shard_map/all_to_all | solution.py:12
  92.8 197.9 %all-gather.5.cloned.1.call-done = bf16[2048,2304]{1,0:T(8,128)(2,1)} async-done(((bf16[256,2304]{1,0:T(8,128)(2,1)}), bf16[2048,2304]{1,0:T(8,128)(2,1)}) %all-gather.5.cloned.1.call-update) | async-done | bytes 9437200 | tf_op jit(solution)/shard_map/all_gather | solution.py:38
  290.7 0.0 all-to-all-done
  290.7 29.3 %convolution_convert_fusion = bf16[2304,2304]{1,0:T(8,128)(2,1)} fusion(bf16[2048,2304]{1,0:T(8,128)(2,1)} %bitcast.9, bf16[2048,2304]{1,0:T(8,128)(2,1)} %all-gather.5.cloned.1.call-done), kind=kOutput, calls=%fused_computation | convolution fusion | flops 21748580352 | bytes 29491200 | tf_op jit(solution)/shard_map/dot_general | solution.py:36
  (1 shorter events, 0.0 us)
Async XLA Ops:
  6.5 64.6 %all-gather.3.cloned.1.call-start = ((), (), s32[]{:S(2)}) async-start(), calls=%async_computation.1 | async-start | bytes 10027008 | tf_op jit(solution)/shard_map/all_gather | solution.py:33
  11.5 279.2 %all-gather.5.cloned.1.call-start = ((), (), s32[]{:S(2)}) async-start(), calls=%async_computation.2 | async-start | bytes 10616832 | tf_op jit(solution)/shard_map/all_gather | solution.py:38
  71.2 10.3 %copy-start = (bf16[256,18432]{1,0:T(8,128)(2,1)S(1)}, bf16[256,18432]{1,0:T(8,128)(2,1)}, u32[]{:S(2)}) copy-start(bf16[256,18432]{1,0:T(8,128)(2,1)} %all-gather.3.cloned.1.call-done) | copy-start | bytes 28311556
  85.9 204.8 %all-to-all-start = ((bf16[8,1,256,2304]{3,2,1,0:T(8,128)(2,1)}), bf16[8,1,256,2304]{3,2,1,0:T(8,128)(2,1)}, u32[]{:S(2)}, u32[]{:S(2)}) async-start(bf16[8,1,256,2304]{3,2,1,0:T(8,128)(2,1)} %fusion), calls=%async_computation | async-start | bytes 18874368 | tf_op jit(solution)/shard_map/all_to_all | solution.py:12
Sparse Core Ops, SparseCore 0:
  11.6 59.4 all-gather.2
  73.5 217.1 all-gather.4
